TPU v7x, 256 devices: a whole 4x4x8 slice. The times are simulated.
256 devices in a mesh: gx: 16 (over z, core), gy: 4 (over y), gz: 4 (over x).
Axes of the slice: x: 4, y: 4, z: 8, core: 2. Of those that a mesh axis runs over, the one named last changes fastest.
Arguments:
- x_start: float32 [32, 32, 64, 512], P(None, 'gx', 'gy', 'gz'), may hold values from -24 to 24
- labels: int32 [32, 64, 512], P('gx', 'gy', 'gz'), may hold values from 0 to 7
- conduct: float32 [8, 9], replicated, may hold values from 0.025 to 4
- electrodes: int32 [33], replicated, may hold values from 0 to 1048575
Outputs:
- lead_fields: float32 [32, 32, 64, 512], P(None, 'gx', 'gy', 'gz')
All inputs are finite; a program needn't handle non-finite values.
Results may differ from a plain program's by a relative error of at most 0.0003.
Values sent between devices are 32-bit elements; how exact they have to be, the bound alone decides.
A program may use at most 64 MiB of HBM per device.

v0:
```python
import jax
import jax.numpy as jnp
from jax import lax
from jax.sharding import PartitionSpec as P

ITERS = 3


LINKS = (
    (0, (1, 0, 0)),
    (1, (0, 1, 0)),
    (2, (0, 0, 1)),
    (3, (1, 1, 0)),
    (4, (1, -1, 0)),
    (5, (1, 0, 1)),
    (6, (1, 0, -1)),
    (7, (0, 1, 1)),
    (8, (0, 1, -1)),
)
HIGH = lax.Precision.HIGHEST


def with_halo(value, sides, width):
    for axis, dim in sides:
        devices, length = (lax.axis_size(axis), value.shape[dim])
        up = [(i, (i + 1) % devices) for i in range(devices - 1)]
        down = [(j, i) for i, j in up]
        last = lax.slice_in_dim(value, length - width, length, axis=dim)
        leading = lax.slice_in_dim(value, 0, width, axis=dim)
        before = lax.ppermute(last, axis, up)
        after = lax.ppermute(leading, axis, down)
        value = jnp.concatenate([before, value, after], axis=dim)
    return value


def neighbour(padded, offset, shape):
    dx, dy, dz = offset
    return padded[
        ..., 1 + dx : 1 + dx + shape[0], 1 + dy : 1 + dy + shape[1], 1 + dz : 1 + dz + shape[2]
    ]


def link_weights(coef, coef_pad):
    shape = coef.shape[1:]
    result = []
    for kind, step in LINKS:
        for sign in (1, -1):
            offset = (sign * step[0], sign * step[1], sign * step[2])
            result.append((offset, 0.5 * (coef[kind] + neighbour(coef_pad[kind], offset, shape))))
    return result


def apply_links(field, padded, weights):
    shape = field.shape[-3:]
    total = jnp.zeros(field.shape, jnp.float32)
    for offset, weight in weights:
        total = total + weight[None] * (field - neighbour(padded, offset, shape))
    return total


def local_gram(first, second):
    count = first.shape[0]
    return jnp.einsum(
        "ri,si->rs", first.reshape(count, -1), second.reshape(count, -1), precision=HIGH
    )


def combine(coeff, field):
    count = field.shape[0]
    return jnp.dot(coeff.T, field.reshape(count, -1), precision=HIGH).reshape(field.shape)


def spd_solve(matrix, right):
    lower = lax.linalg.cholesky(matrix)
    middle = lax.linalg.triangular_solve(lower, right, left_side=True, lower=True)
    return lax.linalg.triangular_solve(lower, middle, left_side=True, lower=True, transpose_a=True)


def extend(field):
    return with_halo(field, (("gx", 1), ("gy", 2), ("gz", 3)), 1)


def per_device(x_start, labels, conduct, electrodes):
    count, cell_x, cell_y, cell_z = x_start.shape
    tissue = conduct.shape[0]
    onehot = (labels[None] == jnp.arange(tissue, dtype=jnp.int32)[:, None, None, None]).astype(
        jnp.float32
    )
    coef = jnp.einsum("lk,lxyz->kxyz", conduct, onehot, precision=HIGH)
    coef_pad = with_halo(coef, (("gx", 1), ("gy", 2), ("gz", 3)), 1)
    weights = link_weights(coef, coef_pad)

    def operate(field):
        return apply_links(field, extend(field), weights)

    span_y = cell_y * lax.axis_size("gy")
    span_z = cell_z * lax.axis_size("gz")
    glob_x = lax.axis_index("gx") * cell_x + jnp.arange(cell_x, dtype=jnp.int32)
    glob_y = lax.axis_index("gy") * cell_y + jnp.arange(cell_y, dtype=jnp.int32)
    glob_z = lax.axis_index("gz") * cell_z + jnp.arange(cell_z, dtype=jnp.int32)
    flat_index = (glob_x[:, None, None] * span_y + glob_y[None, :, None]) * span_z + glob_z[
        None, None, :
    ]
    hits = (flat_index[None] == electrodes[:, None, None, None]).astype(jnp.float32)
    sources = 40.0 * (hits[:count] - hits[count:])
    solution = x_start
    residual = sources - operate(solution)
    direction = residual
    rho = lax.psum(local_gram(residual, residual), ("gx", "gy", "gz"))
    for step in range(ITERS):
        image = operate(direction)
        curvature = lax.psum(local_gram(direction, image), ("gx", "gy", "gz"))
        alpha = spd_solve(curvature, rho)
        solution = solution + combine(alpha, direction)
        if step + 1 < ITERS:
            residual = residual - combine(alpha, image)
            rho_new = lax.psum(local_gram(residual, residual), ("gx", "gy", "gz"))
            beta = spd_solve(rho, rho_new)
            direction = residual + combine(beta, direction)
            rho = rho_new
    return solution


def solution(mesh):
    return jax.shard_map(
        per_device,
        mesh=mesh,
        in_specs=(P(None, "gx", "gy", "gz"), P("gx", "gy", "gz"), P(), P()),
        out_specs=P(None, "gx", "gy", "gz"),
        check_vma=False,
    )
```

profile of v0, /device:TPU:1, one launch (start us, length us, event | category | flops | bytes accessed | tf_op | source)
XLA Modules:
  0.0 601.4 jit_solution(8940108047999747562)
XLA Ops:
  2.1 4.9 collective-permute-start.7
  9.4 3.6 collective-permute-start
  15.2 3.6 collective-permute-done.1
  20.1 4.0 collective-permute-start.2
  26.5 4.0 collective-permute-start.4
  31.4 6.7 %collective-permute-done.5 = f32[9,4,18,1]{3,2,1,0:T(8,128)S(1)} collective-permute-done((f32[9,4,18,1]{3,2,1,0:T(8,128)S(1)}, f32[9,4,18,1]{3,2,1,0:T(8,128)S(1)}, u32[]{:S(2)}, u32[]{:S(2)}) %collective-permute-start.5) | collective-permute-done | bytes 2624 | tf_op jit(solution)/shard_map/ppermute | solution.py:31
  41.9 3.9 collective-permute-start.9
  47.9 2.9 collective-permute-done.8
  54.2 3.8 collective-permute-start.11
  69.5 5.1 collective-permute-start.12
  74.6 4.1 collective-permute-start.13
  83.3 4.0 collective-permute-start.15
  91.7 3.1 collective-permute-start.17
  101.6 2.8 maximum_maximum_fusion.1
  107.4 80.2 %all-reduce = (f32[32,32]{0,1:T(8,128)S(1)}, f32[32,32]{0,1:T(8,128)S(1)}) all-reduce(f32[32,32]{0,1:T(8,128)S(1)} %copy-done.89, f32[32,32]{0,1:T(8,128)S(1)} %convolution_bitcast_fusion.11), channel_id=1, replica_groups=mesh['gx'=16,'gy'=4,'gz'=4] {'gx','gy','gz'}, use_global_device_ids=true, to_apply=%region_3.5 | all-reduce | flops 2048 | bytes 16384 | tf_op jit(solution)/shard_map/psum | solution.py:109
  187.7 2.9 custom-call.21
  196.9 74.4 %psum.44 = f32[32,32]{0,1:T(8,128)S(1)} all-reduce(f32[32,32]{0,1:T(8,128)S(1)} %convolution_bitcast_fusion.8), channel_id=1, replica_groups=mesh['gx'=16,'gy'=4,'gz'=4] {'gx','gy','gz'}, use_global_device_ids=true, to_apply=%region_4.8 | all-reduce | flops 1024 | bytes 8192 | tf_op jit(solution)/shard_map/psum | solution.py:117
  271.3 2.9 custom-call.24
  282.1 3.0 collective-permute-start.19
  285.2 2.9 custom-call.30
  290.1 4.0 collective-permute-start.21
  296.2 3.1 custom-call.32
  314.4 2.8 maximum_maximum_fusion.2
  320.0 76.8 %psum.45 = f32[32,32]{0,1:T(8,128)S(1)} all-reduce(f32[32,32]{0,1:T(8,128)S(1)} %convolution_bitcast_fusion.6), channel_id=1, replica_groups=mesh['gx'=16,'gy'=4,'gz'=4] {'gx','gy','gz'}, use_global_device_ids=true, to_apply=%region_5.9 | all-reduce | flops 1024 | bytes 8192 | tf_op jit(solution)/shard_map/psum | solution.py:112
  396.9 2.9 custom-call.27
  406.0 74.8 %psum.46 = f32[32,32]{1,0:T(8,128)S(1)} all-reduce(f32[32,32]{1,0:T(8,128)S(1)} %convolution_bitcast_fusion.4), channel_id=1, replica_groups=mesh['gx'=16,'gy'=4,'gz'=4] {'gx','gy','gz'}, use_global_device_ids=true, to_apply=%region_6.10 | all-reduce | flops 1024 | bytes 8192 | tf_op jit(solution)/shard_map/psum | solution.py:117
  482.1 2.6 collective-permute-start.24
  484.7 3.0 collective-permute-start.25
  492.3 4.0 collective-permute-start.27
  511.8 3.6 convolution_bitcast_fusion.2
  515.4 76.4 %psum.47 = f32[32,32]{0,1:T(8,128)S(1)} all-reduce(f32[32,32]{0,1:T(8,128)S(1)} %convolution_bitcast_fusion.2), channel_id=1, replica_groups=mesh['gx'=16,'gy'=4,'gz'=4] {'gx','gy','gz'}, use_global_device_ids=true, to_apply=%region_7.11 | all-reduce | flops 1024 | bytes 8192 | tf_op jit(solution)/shard_map/psum | solution.py:112
  591.9 2.9 custom-call.33
  (360 shorter events, 119.2 us)
Async XLA Ops:
  2.1 39.0 %collective-permute-start.7 = (f32[32,1,16,128]{3,0,2,1:T(8,128)S(1)}, f32[32,1,16,128]{3,0,2,1:T(8,128)S(1)}, u32[]{:S(2)}, u32[]{:S(2)}) collective-permute-start(f32[32,1,16,128]{3,0,2,1:T(8,128)S(1)} %get-tuple-element.56), channel_id=1, source_target_pairs={{0,16},{16,32},{32,48},{48,64},{64,80},{80,96},{96,112},{112,128},... | collective-permute-start | bytes 786440 | tf_op jit(solution)/shard_map/ppermute | solution.py:30
  7.0 34.8 %collective-permute-start.6 = (f32[32,1,16,128]{3,0,2,1:T(8,128)}, f32[32,1,16,128]{3,0,2,1:T(8,128)S(1)}, u32[]{:S(2)}, u32[]{:S(2)}) collective-permute-start(f32[32,1,16,128]{3,0,2,1:T(8,128)} %get-tuple-element.55), channel_id=1, source_target_pairs={{16,0},{32,16},{48,32},{64,48},{80,64},{96,80},{112,96},{128,112},... | collective-permute-start | bytes 786440 | tf_op jit(solution)/shard_map/ppermute | solution.py:31
  9.4 5.7 collective-permute-start
  13.0 5.7 collective-permute-start.1
  18.8 5.4 collective-permute-start.3
  20.1 4.9 collective-permute-start.2
  25.2 12.9 %collective-permute-start.5 = (f32[9,4,18,1]{3,2,1,0:T(8,128)S(1)}, f32[9,4,18,1]{3,2,1,0:T(8,128)S(1)}, u32[]{:S(2)}, u32[]{:S(2)}) collective-permute-start(f32[9,4,18,1]{3,2,1,0:T(8,128)S(1)} %get-tuple-element.58), channel_id=1, source_target_pairs={{1,0},{2,1},{3,2},{5,4},{6,5},{7,6},{9,8},{10,9},{11,10},{13,12},{... | collective-permute-start | bytes 7784 | tf_op jit(solution)/shard_map/ppermute | solution.py:31
  26.5 13.3 %collective-permute-start.4 = (f32[9,4,18,1]{3,2,1,0:T(8,128)S(1)}, f32[9,4,18,1]{3,2,1,0:T(8,128)S(1)}, u32[]{:S(2)}, u32[]{:S(2)}) collective-permute-start(f32[9,4,18,1]{3,2,1,0:T(8,128)S(1)} %get-tuple-element.57), channel_id=1, source_target_pairs={{0,1},{1,2},{2,3},{4,5},{5,6},{6,7},{8,9},{9,10},{10,11},{12,13},{... | collective-permute-start | bytes 7784 | tf_op jit(solution)/shard_map/ppermute | solution.py:30
  41.9 6.0 collective-permute-start.9
  45.8 5.0 collective-permute-start.8
  54.2 7.2 %collective-permute-start.11 = (f32[32,4,18,1]{0,1,3,2:T(4,128)S(1)}, f32[32,4,18,1]{0,1,3,2:T(4,128)S(1)}, u32[]{:S(2)}, u32[]{:S(2)}) collective-permute-start(f32[32,4,18,1]{0,1,3,2:T(4,128)S(1)} %copy.135), channel_id=1, source_target_pairs={{0,1},{1,2},{2,3},{4,5},{5,6},{6,7},{8,9},{9,10},{10,11},{12,13},{... | collective-permute-start | bytes 27656 | tf_op jit(solution)/shard_map/ppermute | solution.py:30
  58.5 4.7 collective-permute-start.10
  69.5 11.4 %collective-permute-start.12 = (f32[32,1,16,128]{3,0,2,1:T(8,128)S(1)}, f32[32,1,16,128]{3,0,2,1:T(8,128)S(1)}, u32[]{:S(2)}, u32[]{:S(2)}) collective-permute-start(f32[32,1,16,128]{3,0,2,1:T(8,128)S(1)} %get-tuple-element.54), channel_id=1, source_target_pairs={{16,0},{32,16},{48,32},{64,48},{80,64},{96,80},{112,96},{128,112},... | collective-permute-start | bytes 786440 | tf_op jit(solution)/shard_map/ppermute | solution.py:31
  74.6 7.4 %collective-permute-start.13 = (f32[32,1,16,128]{3,0,2,1:T(8,128)S(1)}, f32[32,1,16,128]{3,0,2,1:T(8,128)S(1)}, u32[]{:S(2)}, u32[]{:S(2)}) collective-permute-start(f32[32,1,16,128]{3,0,2,1:T(8,128)S(1)} %get-tuple-element.53), channel_id=1, source_target_pairs={{0,16},{16,32},{32,48},{48,64},{64,80},{80,96},{96,112},{112,128},... | collective-permute-start | bytes 786440 | tf_op jit(solution)/shard_map/ppermute | solution.py:30
  82.0 8.0 %collective-permute-start.14 = (f32[32,4,1,128]{3,0,2,1:T(8,128)S(1)}, f32[32,4,1,128]{3,0,2,1:T(8,128)S(1)}, u32[]{:S(2)}, u32[]{:S(2)}) collective-permute-start(f32[32,4,1,128]{3,0,2,1:T(8,128)S(1)} %get-tuple-element.37), channel_id=1, source_target_pairs={{4,0},{8,4},{12,8},{5,1},{9,5},{13,9},{6,2},{10,6},{14,10},{7,3},{... | collective-permute-start | bytes 196616 | tf_op jit(solution)/shard_map/ppermute | solution.py:31
  83.3 6.7 %collective-permute-start.15 = (f32[32,4,1,128]{3,0,2,1:T(8,128)S(1)}, f32[32,4,1,128]{3,0,2,1:T(8,128)S(1)}, u32[]{:S(2)}, u32[]{:S(2)}) collective-permute-start(f32[32,4,1,128]{3,0,2,1:T(8,128)S(1)} %get-tuple-element.36), channel_id=1, source_target_pairs={{0,4},{4,8},{8,12},{1,5},{5,9},{9,13},{2,6},{6,10},{10,14},{3,7},{... | collective-permute-start | bytes 196616 | tf_op jit(solution)/shard_map/ppermute | solution.py:30
  91.7 5.7 collective-permute-start.17
  95.3 4.7 collective-permute-start.16
  279.6 9.2 %collective-permute-start.18 = (f32[32,1,16,128]{3,0,2,1:T(8,128)S(1)}, f32[32,1,16,128]{3,0,2,1:T(8,128)S(1)}, u32[]{:S(2)}, u32[]{:S(2)}) collective-permute-start(f32[32,1,16,128]{3,0,2,1:T(8,128)S(1)} %get-tuple-element.52), channel_id=1, source_target_pairs={{16,0},{32,16},{48,32},{64,48},{80,64},{96,80},{112,96},{128,112},... | collective-permute-start | bytes 786440 | tf_op jit(solution)/shard_map/ppermute | solution.py:31
  282.1 6.6 %collective-permute-start.19 = (f32[32,1,16,128]{3,0,2,1:T(8,128)S(1)}, f32[32,1,16,128]{3,0,2,1:T(8,128)S(1)}, u32[]{:S(2)}, u32[]{:S(2)}) collective-permute-start(f32[32,1,16,128]{3,0,2,1:T(8,128)S(1)} %get-tuple-element.51), channel_id=1, source_target_pairs={{0,16},{16,32},{32,48},{48,64},{64,80},{80,96},{96,112},{112,128},... | collective-permute-start | bytes 786440 | tf_op jit(solution)/shard_map/ppermute | solution.py:30
  288.8 10.5 %collective-permute-start.20 = (f32[32,4,1,128]{3,0,2,1:T(8,128)S(1)}, f32[32,4,1,128]{3,0,2,1:T(8,128)S(1)}, u32[]{:S(2)}, u32[]{:S(2)}) collective-permute-start(f32[32,4,1,128]{3,0,2,1:T(8,128)S(1)} %get-tuple-element.33), channel_id=1, source_target_pairs={{4,0},{8,4},{12,8},{5,1},{9,5},{13,9},{6,2},{10,6},{14,10},{7,3},{... | collective-permute-start | bytes 196616 | tf_op jit(solution)/shard_map/ppermute | solution.py:31
  290.1 9.2 %collective-permute-start.21 = (f32[32,4,1,128]{3,0,2,1:T(8,128)S(1)}, f32[32,4,1,128]{3,0,2,1:T(8,128)S(1)}, u32[]{:S(2)}, u32[]{:S(2)}) collective-permute-start(f32[32,4,1,128]{3,0,2,1:T(8,128)S(1)} %get-tuple-element.32), channel_id=1, source_target_pairs={{0,4},{4,8},{8,12},{1,5},{5,9},{9,13},{2,6},{6,10},{10,14},{3,7},{... | collective-permute-start | bytes 196616 | tf_op jit(solution)/shard_map/ppermute | solution.py:30
  303.0 7.0 %collective-permute-start.23 = (f32[32,4,18,1]{0,1,3,2:T(4,128)S(1)}, f32[32,4,18,1]{0,1,3,2:T(4,128)S(1)}, u32[]{:S(2)}, u32[]{:S(2)}) collective-permute-start(f32[32,4,18,1]{0,1,3,2:T(4,128)S(1)} %copy.175), channel_id=1, source_target_pairs={{0,1},{1,2},{2,3},{4,5},{5,6},{6,7},{8,9},{9,10},{10,11},{12,13},{... | collective-permute-start | bytes 27656 | tf_op jit(solution)/shard_map/ppermute | solution.py:30
  307.2 4.8 collective-permute-start.22
  482.1 7.7 %collective-permute-start.24 = (f32[32,1,16,128]{3,0,2,1:T(8,128)S(1)}, f32[32,1,16,128]{3,0,2,1:T(8,128)S(1)}, u32[]{:S(2)}, u32[]{:S(2)}) collective-permute-start(f32[32,1,16,128]{3,0,2,1:T(8,128)S(1)} %get-tuple-element.50), channel_id=1, source_target_pairs={{16,0},{32,16},{48,32},{64,48},{80,64},{96,80},{112,96},{128,112},... | collective-permute-start | bytes 786440 | tf_op jit(solution)/shard_map/ppermute | solution.py:31
  484.7 6.3 %collective-permute-start.25 = (f32[32,1,16,128]{3,0,2,1:T(8,128)S(1)}, f32[32,1,16,128]{3,0,2,1:T(8,128)S(1)}, u32[]{:S(2)}, u32[]{:S(2)}) collective-permute-start(f32[32,1,16,128]{3,0,2,1:T(8,128)S(1)} %get-tuple-element.49), channel_id=1, source_target_pairs={{0,16},{16,32},{32,48},{48,64},{64,80},{80,96},{96,112},{112,128},... | collective-permute-start | bytes 786440 | tf_op jit(solution)/shard_map/ppermute | solution.py:30
  491.0 8.5 %collective-permute-start.26 = (f32[32,4,1,128]{3,0,2,1:T(8,128)S(1)}, f32[32,4,1,128]{3,0,2,1:T(8,128)S(1)}, u32[]{:S(2)}, u32[]{:S(2)}) collective-permute-start(f32[32,4,1,128]{3,0,2,1:T(8,128)S(1)} %get-tuple-element.29), channel_id=1, source_target_pairs={{4,0},{8,4},{12,8},{5,1},{9,5},{13,9},{6,2},{10,6},{14,10},{7,3},{... | collective-permute-start | bytes 196616 | tf_op jit(solution)/shard_map/ppermute | solution.py:31
  492.3 7.2 %collective-permute-start.27 = (f32[32,4,1,128]{3,0,2,1:T(8,128)S(1)}, f32[32,4,1,128]{3,0,2,1:T(8,128)S(1)}, u32[]{:S(2)}, u32[]{:S(2)}) collective-permute-start(f32[32,4,1,128]{3,0,2,1:T(8,128)S(1)} %get-tuple-element.28), channel_id=1, source_target_pairs={{0,4},{4,8},{8,12},{1,5},{5,9},{9,13},{2,6},{6,10},{10,14},{3,7},{... | collective-permute-start | bytes 196616 | tf_op jit(solution)/shard_map/ppermute | solution.py:30
  501.2 5.6 collective-permute-start.29
  503.8 4.8 collective-permute-start.28
  511.7 87.4 %copy-start.11 = (f32[32,2,16,128]{3,0,2,1:T(8,128)S(1)}, f32[32,2,16,128]{3,0,2,1:T(8,128)}, u32[]{:S(2)}) copy-start(f32[32,2,16,128]{3,0,2,1:T(8,128)} %convolution_add_fusion.2) | copy-start | bytes 1572868
  511.8 87.4 %copy-start.12 = (f32[4,8,32,128]{3,2,1,0:T(8,128)S(1)}, f32[4,8,32,128]{3,2,1,0:T(8,128)}, u32[]{:S(2)}) copy-start(f32[4,8,32,128]{3,2,1,0:T(8,128)} %copy.231) | copy-start | bytes 1572868
  (91 other events, 580.8 us)
where the time goes:
time: 610 us; the launch traced here: 601 us
  blocking collectives  383 us (63%)
  starting transfers between devices  81.7 us (13%)
  other arithmetic  56.3 us (9%)
  local copies, waits for them, and re-layouts  36.3 us (6%)
  waiting for transfers between devices  25.5 us (4%)
  matrix products  16.6 us (3%)
    psum x2, blocking collectives, per_device(): curvature = lax.psum(local_gram(direction, image), ('gx', 'gy', 'gz'))  153 us
    psum x2, blocking collectives, per_device(): rho_new = lax.psum(local_gram(residual, residual), ('gx', 'gy', 'gz'))  149 us
    psum x1, blocking collectives, per_device(): rho = lax.psum(local_gram(residual, residual), ('gx', 'gy', 'gz'))  80.2 us
    ppermute x15, starting transfers between devices, with_halo(): before = lax.ppermute(last, axis, up)  54 us
    ppermute x15, starting transfers between devices, with_halo(): after = lax.ppermute(leading, axis, down)  27.7 us
    ppermute x15, waiting for transfers between devices, with_halo(): after = lax.ppermute(leading, axis, down)  20.5 us
    another operation x15, other arithmetic, spd_solve(): lower = lax.linalg.cholesky(matrix)  18.2 us
    another operation x10, other arithmetic, spd_solve(): lax.linalg.triangular_solve(lower, middle, left_side=True, lower=True, tr...  16.2 us
  transfers between devices with their start and end apart: 30, of which 13 were waited for; matrix products, arithmetic and copies ran while one was open for 5% of the time, Pallas kernels for 0%

commit v1 on v0

v1 whole, which is shorter than its diff:
```python
import jax
import jax.numpy as jnp
from jax import lax
from jax.experimental import pallas as pl
from jax.experimental.pallas import tpu as pltpu
from jax.sharding import PartitionSpec as P

NRHS, LABELS = 32, 8
CX, CY, CZ = 2, 16, 128
GX, GY, GZ = 16, 4, 4
CELLS = CX * CY
F32 = jnp.float32
HIGH = lax.Precision.HIGHEST
MESH = pl.DeviceIdType.MESH

KINDS = {}
for kind, step in enumerate(
    ((1, 0, 0), (0, 1, 0), (0, 0, 1), (1, 1, 0), (1, -1, 0), (1, 0, 1), (1, 0, -1), (0, 1, 1), (0, 1, -1))
):
    KINDS[step] = kind
    KINDS[tuple(-s for s in step)] = kind
NEAR = sorted(KINDS)
CROSS = ((0, 0), (1, 0), (-1, 0), (0, 1), (0, -1))
FLAT = tuple(o for o in NEAR if o[2] == 0)
SIDE = tuple(o for o in NEAR if o[2] != 0)
PLANE = tuple((0, b, c) for b in range(GY) for c in range(GZ) if b or c)
LINE = tuple((2 * a, 0, 0) for a in range(1, GX // 2))
HALO_TILES = 90
LABEL_TILES = 36


def wrapped(offset):
    return (offset[0] % GX, offset[1] % GY, offset[2] % GZ)


def coordinates():
    return lax.axis_index("gx"), lax.axis_index("gy"), lax.axis_index("gz")


def device(offset):
    x, y, z = coordinates()
    dx, dy, dz = wrapped(offset)
    return (lax.rem(x + dx, GX), lax.rem(y + dy, GY), lax.rem(z + dz, GZ))


def from_slot(offset, order):
    return order.index(tuple(-o for o in offset))


def mm(a, b):
    return jnp.dot(a, b, precision=HIGH, preferred_element_type=F32)


def mm_t(a, b):
    return lax.dot_general(a, b, (((0,), (0,)), ((), ())), precision=HIGH, preferred_element_type=F32)


def mm_nt(a, b):
    return lax.dot_general(a, b, (((1,), (1,)), ((), ())), precision=HIGH, preferred_element_type=F32)


def lanes(shape):
    return lax.broadcasted_iota(jnp.int32, shape, 1)


def sublanes(shape):
    return lax.broadcasted_iota(jnp.int32, shape, 0)


def eliminate(matrix):
    tiles = [matrix[8 * g : 8 * g + 8] for g in range(4)]
    row = sublanes((8, 128))
    width = 8
    for start in range(0, NRHS, width):
        columns = [
            [jnp.broadcast_to(t[:, start + j : start + j + 1], (8, 128)) for t in tiles] for j in range(width)
        ]
        for j in range(width):
            own, inner = divmod(start + j, 8)
            scale = 1.0 / columns[j][own][inner : inner + 1]
            for which in [None] + list(range(j + 1, width)):
                target = tiles if which is None else columns[which]
                pivot = jnp.broadcast_to(target[own][inner : inner + 1] * scale, (8, 128))
                new = [t - c * pivot for t, c in zip(target, columns[j])]
                new[own] = jnp.where(row == inner, pivot, new[own])
                if which is None:
                    tiles = new
                else:
                    columns[which] = new
    return jnp.concatenate(tiles, axis=0)


def part(matrix, index):
    if index:
        matrix = pltpu.roll(matrix, 128 - 32 * index, 1)
    return matrix[:, :NRHS]


def lookup(label, conduct, kind):
    value = jnp.zeros(label.shape, F32)
    for tissue in range(LABELS):
        value = jnp.where(label == tissue, conduct[tissue, kind], value)
    return value


def kernel(
    x_ref, label_ref, conduct, electrodes, out_ref,
    f0, f1, f2, f3, f4, dirs, image, second,
    label_got, padded, rows, weights, side_weights,
    pack0, pack1, pack2, pack3, got0, got1, got2, got3, ends,
    give, plane_a, line_a, pair_a, mid_a, sum_a, plane_b, line_b, pair_b, mid_b, sum_b,
    dummy, halo_send, halo_recv, label_sem, red_send, red_recv,
):
    fields = (f0, f1, f2, f3)
    packs = (pack0, pack1, pack2, pack3)
    gots = (got0, got1, got2, got3)
    gx, gy, gz = coordinates()
    lane8 = lanes((8, 128))

    partners = list(dict.fromkeys([wrapped(o) for o in NEAR] + list(PLANE) + list(LINE)))
    barrier = pltpu.get_barrier_semaphore()
    for offset in partners:
        pl.semaphore_signal(barrier, inc=1, device_id=device(offset), device_id_type=MESH)
    pl.semaphore_wait(barrier, len(partners))

    def put(src, dst, send, recv, offset):
        pltpu.make_async_remote_copy(
            src_ref=src, dst_ref=dst, send_sem=send, recv_sem=recv,
            device_id=device(offset), device_id_type=MESH,
        ).start()

    def take(ref, sem):
        pltpu.make_async_copy(ref, ref, sem).wait()

    def label_part(ref, offset):
        dx, dy, _ = offset
        xs = {0: pl.ds(0, CX), 1: pl.ds(CX - 1, 1), -1: pl.ds(0, 1)}[dx]
        ys = {0: pl.ds(0, CY), 1: pl.ds(CY - 8, 8), -1: pl.ds(0, 8)}[dy]
        return ref.at[xs, ys]

    for slot, offset in enumerate(NEAR):
        put(label_part(label_ref, offset), label_part(label_got.at[slot], offset), label_sem.at[0], label_sem.at[1], offset)

    def send(level, chunk):
        field, pack, got = fields[level], packs[level], gots[level]
        r = pl.ds(16 * chunk, 16)
        ss, rs = halo_send.at[level, chunk], halo_recv.at[level, chunk]
        x_from, x_to = {1: CX, -1: 1}, {1: 0, -1: CX + 1}
        y_from, y_to = {1: CY, -1: 1}, {1: 0, -1: CY + 1}
        for dx in (1, -1):
            put(field.at[x_from[dx], 1 : CY + 1, r], field.at[x_to[dx], 1 : CY + 1, r], ss, rs, (dx, 0, 0))
        for slot, offset in enumerate(SIDE):
            put(pack.at[chunk], got.at[slot, chunk], ss, rs, offset)
        for dy in (1, -1):
            put(field.at[1 : CX + 1, y_from[dy], r], field.at[1 : CX + 1, y_to[dy], r], ss, rs, (0, dy, 0))
        for dx in (1, -1):
            for dy in (1, -1):
                put(field.at[x_from[dx], y_from[dy], r], field.at[x_to[dx], y_to[dy], r], ss, rs, (dx, dy, 0))

    for chunk in range(2):

        def load(y, acc, chunk=chunk):
            for x in range(CX):
                tile = x_ref[pl.ds(512 * chunk + CY * x + y, 16, stride=CELLS), :]
                f0[x + 1, y + 1, 16 * chunk : 16 * chunk + 16, :] = tile
                for half in range(2):
                    spot = 32 * half + CY * x + y
                    acc = jnp.where(lane8 // 2 == spot, pltpu.roll(tile[8 * half : 8 * half + 8], 2 * spot + 1, 1), acc)
            return acc

        pack0[chunk] = lax.fori_loop(0, CY, load, jnp.zeros((8, 128), F32))
        send(0, chunk)

    take(dummy.at[pl.ds(0, LABEL_TILES)], label_sem.at[1])
    lane16 = lanes((CY, 128))
    inside = {
        (0, 1): gx < GX - 1, (0, -1): gx > 0, (1, 1): gy < GY - 1, (1, -1): gy > 0, (2, 1): gz < GZ - 1, (2, -1): gz > 0,
    }

    def block(offset, x, top):
        ref = label_ref if offset == (0, 0, 0) else label_got.at[from_slot(offset, NEAR)]
        if top is None:
            return ref[x]
        return ref[x, CY - 8 : CY] if top < 0 else ref[x, 0:8]

    def put_rows(shift, xx, dx, dy):
        x = {0: xx - 1, 1: 0, -1: CX - 1}[dx]
        value = block((dx, dy, 0), x, dy or None)
        lane = lanes(value.shape)
        if shift:
            other = block((dx, dy, shift), x, dy or None)
            other = jnp.where(inside[2, shift], other, -1)
            edge = 127 if shift == 1 else 0
            value = jnp.where(lane == edge, pltpu.roll(other, (-shift) % 128, 1), pltpu.roll(value, (-shift) % 128, 1))
        if dx:
            value = jnp.where(inside[0, dx], value, -1)
        if dy:
            value = jnp.where(inside[1, dy], value, -1)
        row = {0: 8, 1: 24, -1: 0}[dy]
        padded[shift + 1, xx, row : row + value.shape[0], :] = value

    for shift in (0, 1, -1):
        for xx in range(CX + 2):
            dx = -1 if xx == 0 else (1 if xx == CX + 1 else 0)
            put_rows(shift, xx, dx, 0)
            if dx == 0 or shift == 0:
                put_rows(shift, xx, dx, 1)
                put_rows(shift, xx, dx, -1)

    for x in range(CX):
        here = padded[1, x + 1, 8:24, :]
        own = [lookup(here, conduct, kind) for kind in range(9)]
        total = jnp.zeros((CY, 128), F32)
        for offset in NEAR:
            dx, dy, dz = offset
            there = padded[dz + 1, x + 1 + dx, 8 + dy : 24 + dy, :]
            kind = KINDS[offset]
            weight = 0.5 * (own[kind] + lookup(there, conduct, kind))
            total = total + weight
            weight = jnp.where(there >= 0, weight, 0.0)
            if dz:
                weight = pltpu.roll(weight, dz % 128, 1)
                index = 9 + 5 * (dz < 0) + CROSS.index((dx, dy))
            else:
                index = 1 + FLAT.index(offset)
            rows[index, CY * x : CY * x + CY, :] = weight
        rows[0, CY * x : CY * x + CY, :] = total

    def spread(c, carry):
        for index in range(19):
            weights[index, c] = jnp.broadcast_to(rows[index, pl.ds(c, 1), :], (8, 128))
        return carry

    lax.fori_loop(0, CELLS, spread, 0)

    pair_lane = lanes((CELLS, 128))
    keep = (pair_lane % 64) // 2 == sublanes((CELLS, 128))
    for f in range(5):
        up = jnp.broadcast_to(rows[9 + f][:, 0:1], (CELLS, 128))
        down = jnp.broadcast_to(rows[14 + f][:, 127:128], (CELLS, 128))
        both = jnp.where(keep, jnp.where(pair_lane % 2 == 1, up, down), 0.0)
        side_weights[f] = jnp.broadcast_to(jnp.sum(both, axis=0, keepdims=True), (8, 128))

    flat_base = gx * (CX * GY * CY * GZ * CZ) + gy * (CY * GZ * CZ) + gz * CZ
    row8 = sublanes((8, 128))
    wanted = []
    for g in range(4):
        tile = jnp.zeros((8, 128), jnp.int32)
        for i in range(8):
            tile = jnp.where(row8 == i, electrodes[8 * g + i], tile)
        wanted.append(tile)
    common = electrodes[NRHS]

    def operate(level, chunk):
        src, got, base = fields[level], gots[level], 16 * chunk
        dst = f4 if level == 3 else fields[level + 1]

        def sides(dx, dy):
            up = got[from_slot((dx, dy, 1), SIDE), chunk]
            down = got[from_slot((dx, dy, -1), SIDE), chunk]
            return jnp.where(lane8 % 2 == 1, up, down)

        center = sides(0, 0)
        cell_x, cell_y = (lane8 % 64) // 32, (lane8 % 32) // 2
        parts = {
            (0, 0): center,
            (1, 0): jnp.where(cell_x == 1, pltpu.roll(sides(1, 0), 32, 1), pltpu.roll(center, 96, 1)),
            (-1, 0): jnp.where(cell_x == 0, pltpu.roll(sides(-1, 0), 96, 1), pltpu.roll(center, 32, 1)),
            (0, 1): jnp.where(cell_y == 15, pltpu.roll(sides(0, 1), 30, 1), pltpu.roll(center, 126, 1)),
            (0, -1): jnp.where(cell_y == 0, pltpu.roll(sides(0, -1), 98, 1), pltpu.roll(center, 2, 1)),
        }
        end = jnp.zeros((8, 128), F32)
        for f, cross in enumerate(CROSS):
            end = end + side_weights[f] * parts[cross]
        ends[...] = end

        def body(y, acc):
            results = []
            for x in range(CX):
                c = CY * x + y
                for half in range(2):
                    r = pl.ds(base + 8 * half, 8)
                    u = {
                        (dx, dy): src[x + 1 + dx, y + 1 + dy, r, :] for dx in (-1, 0, 1) for dy in (-1, 0, 1)
                    }
                    value = weights[0, c] * u[0, 0]
                    for i, offset in enumerate(FLAT):
                        value = value - weights[1 + i, c] * u[offset[0], offset[1]]
                    up = weights[9, c] * u[0, 0]
                    down = weights[14, c] * u[0, 0]
                    for f in range(1, 5):
                        up = up + weights[9 + f, c] * u[CROSS[f]]
                        down = down + weights[14 + f, c] * u[CROSS[f]]
                    spot = 32 * half + c
                    side = pltpu.roll(ends[...], 127 - 2 * spot, 1)
                    up = jnp.where(lane8 == 0, side, up)
                    down = jnp.where(lane8 == 127, side, down)
                    value = value - pltpu.roll(up, 127, 1) - pltpu.roll(down, 1, 1)
                    if level == 0:
                        flat = flat_base + x * (GY * CY * GZ * CZ) + y * (GZ * CZ) + lane8
                        hit = jnp.where(flat == wanted[2 * chunk + half], 40.0, 0.0)
                        value = (hit - jnp.where(flat == common, 40.0, 0.0)) - value
                    if level < 3:
                        acc = jnp.where(lane8 // 2 == spot, pltpu.roll(value, 2 * spot + 1, 1), acc)
                    results.append((x, r, value))
            for x, r, value in results:
                if level == 3:
                    dst[x, y, r, :] = value
                else:
                    dst[x + 1, y + 1, r, :] = value
            return acc

        acc = lax.fori_loop(0, CY, body, jnp.zeros((8, 128), F32))
        if level < 3:
            packs[level + 1][chunk] = acc

    def arrived(level, chunk):
        take(dummy, halo_recv.at[level, chunk])

    mine = gy * GZ + gz
    chip = gx // 2

    def plane_send(value, got, index):
        give[index] = value.reshape(4, 8, 128)
        got[mine] = value.reshape(4, 8, 128)
        for offset in PLANE:
            put(give.at[index], got.at[mine], red_send.at[index, 0], red_recv.at[index, 0], offset)

    def line_send(plane, got, mid, index):
        take(plane.at[0:15], red_recv.at[index, 0])
        value = plane[0]
        for i in range(1, 16):
            value = value + plane[i]
        mid[0] = value
        got[chip] = value
        for offset in LINE:
            put(mid.at[0], got.at[chip], red_send.at[index, 1], red_recv.at[index, 1], offset)

    def pair_send(line, got, mid, index):
        take(line.at[0:7], red_recv.at[index, 1])
        value = line[0]
        for i in range(1, 8):
            value = value + line[i]
        mid[1] = value
        pltpu.make_async_remote_copy(
            src_ref=mid.at[1], dst_ref=got, send_sem=red_send.at[index, 2], recv_sem=red_recv.at[index, 2],
            device_id=(gx + 1 - 2 * lax.rem(gx, 2), gy, gz), device_id_type=MESH,
        ).start()

    def pair_take(got, mid, index):
        take(got, red_recv.at[index, 2])
        return (mid[1] + got[...]).reshape(NRHS, 128)

    def field_rows(ref, y, inner):
        o = 1 if inner else 0
        return jnp.concatenate([ref[x + o, 2 * y + j + o] for j in range(2) for x in range(CX)], axis=1)

    for level in range(2):
        for chunk in range(2):
            arrived(level, chunk)
            operate(level, chunk)
            send(level + 1, chunk)

    def gram_first(y, acc):
        both = jnp.concatenate([field_rows(f1, y, True), field_rows(f2, y, True)], axis=0)
        return acc + mm_nt(both, both)

    both = lax.fori_loop(0, CY // 2, gram_first, jnp.zeros((64, 64), F32))
    wide = jnp.concatenate([both, jnp.zeros((64, 64), F32)], axis=1)
    lane32 = lanes((NRHS, 128))
    first = jnp.where(lane32 < 64, wide[:NRHS], pltpu.roll(wide[NRHS:], 32, 1))
    first = jnp.where(lane32 < 96, first, 0.0)
    plane_send(first, plane_a, 0)

    arrived(2, 0)
    operate(2, 0)
    send(3, 0)
    line_send(plane_a, line_a, mid_a, 0)
    arrived(2, 1)
    operate(2, 1)
    send(3, 1)
    pair_send(line_a, pair_a, mid_a, 0)
    arrived(3, 0)
    operate(3, 0)
    sums = pair_take(pair_a, mid_a, 0)

    solved = eliminate(pltpu.roll(sums, 96, 1))
    alpha0 = part(solved, 3)
    turn0 = mm(part(solved, 1), alpha0)
    eye = jnp.where(sublanes((NRHS, NRHS)) == lanes((NRHS, NRHS)), 1.0, 0.0)
    beta0 = turn0 - eye
    rho1 = mm(part(sums, 0), beta0)
    mix = jnp.concatenate([turn0, -alpha0], axis=0)

    arrived(3, 1)
    operate(3, 1)

    def second_block(y, acc):
        v0, u1 = field_rows(f1, y, True), field_rows(f2, y, True)
        u2, u3 = field_rows(f3, y, True), field_rows(f4, y, False)
        top = jnp.concatenate([v0, u1, u2], axis=1)
        low = jnp.concatenate([u1, u2, u3], axis=1)
        new = mm_t(mix, jnp.concatenate([top, low], axis=0))
        p1, q1, aq1 = new[:, :512], new[:, 512:1024], new[:, 1024:]
        dirs[y] = p1
        image[y] = q1
        return acc + mm_nt(q1, jnp.concatenate([p1, q1, aq1, u1], axis=0))

    grams = lax.fori_loop(0, CY // 2, second_block, jnp.zeros((NRHS, 128), F32))
    plane_send(grams, plane_b, 1)
    line_send(plane_b, line_b, mid_b, 1)
    pair_send(line_b, pair_b, mid_b, 1)
    sums = pair_take(pair_b, mid_b, 1)

    wide_rho = jnp.concatenate([rho1, jnp.zeros((NRHS, 96), F32)], axis=1)
    solved = eliminate(jnp.where(lane32 < 64, sums, pltpu.roll(wide_rho, 64, 1)))
    alpha1 = part(solved, 2)
    turn1 = mm(part(solved, 1), alpha1)
    qq, qaq, qu = part(sums, 1), part(sums, 2), part(sums, 3)
    gram2 = mm_t(alpha1, mm(qaq, alpha1) + mm(qu, beta0) - mm(qq, turn1))
    rho2 = mm(rho1, turn1 - eye)
    solved = eliminate(jnp.concatenate([gram2, rho2, jnp.zeros((NRHS, 64), F32)], axis=1))
    alpha2 = part(solved, 1)
    last = jnp.concatenate(
        [alpha0 - mm(beta0, alpha2), alpha1 + mm(turn1, alpha2), -mm(alpha1, alpha2)], axis=0
    )

    def finish(y, carry):
        update = mm_t(last, jnp.concatenate([field_rows(f1, y, True), dirs[y], image[y]], axis=0))
        for j in range(2):
            for x in range(CX):
                piece = update[:, 128 * (2 * j + x) : 128 * (2 * j + x) + 128]
                value = f0[x + 1, 2 * y + j + 1] + piece
                out_ref[pl.ds(CY * x + 2 * y + j, NRHS, stride=CELLS), :] = value
        return carry

    lax.fori_loop(0, CY // 2, finish, 0)

    take(dummy.at[pl.ds(0, LABEL_TILES)], label_sem.at[0])
    for level in range(4):
        for chunk in range(2):
            take(dummy, halo_send.at[level, chunk])
    for index, (plane, line, pair) in enumerate(((plane_a, line_a, pair_a), (plane_b, line_b, pair_b))):
        take(plane.at[0:15], red_send.at[index, 0])
        take(line.at[0:7], red_send.at[index, 1])
        take(pair, red_send.at[index, 2])


def per_device(x_start, labels, conduct, electrodes):
    vmem = pl.BlockSpec(memory_space=pltpu.VMEM)
    smem = pl.BlockSpec(memory_space=pltpu.SMEM)
    field = pltpu.VMEM((CX + 2, CY + 2, NRHS, 128), F32)
    half = pltpu.VMEM((CY // 2, NRHS, 512), F32)
    pack = pltpu.VMEM((2, 8, 128), F32)
    got = pltpu.VMEM((10, 2, 8, 128), F32)
    reduce = [
        pltpu.VMEM((16, 4, 8, 128), F32),
        pltpu.VMEM((8, 4, 8, 128), F32),
        pltpu.VMEM((4, 8, 128), F32),
        pltpu.VMEM((2, 4, 8, 128), F32),
        pltpu.VMEM((4, 8, 128), F32),
    ]
    out = pl.pallas_call(
        kernel,
        out_shape=jax.ShapeDtypeStruct((NRHS * CELLS, 128), F32),
        in_specs=[vmem, vmem, smem, smem],
        out_specs=vmem,
        scratch_shapes=[field] * 4
        + [pltpu.VMEM((CX, CY, NRHS, 128), F32), half, half, half]
        + [
            pltpu.VMEM((18, CX, CY, 128), jnp.int32),
            pltpu.VMEM((3, CX + 2, 32, 128), jnp.int32),
            pltpu.VMEM((19, CELLS, 128), F32),
            pltpu.VMEM((19, CELLS, 8, 128), F32),
            pltpu.VMEM((5, 8, 128), F32),
        ]
        + [pack] * 4
        + [got] * 4
        + [pltpu.VMEM((8, 128), F32), pltpu.VMEM((2, 4, 8, 128), F32)]
        + reduce * 2
        + [
            pltpu.VMEM((HALO_TILES, 8, 128), F32),
            pltpu.SemaphoreType.DMA((4, 2)),
            pltpu.SemaphoreType.DMA((4, 2)),
            pltpu.SemaphoreType.DMA((2,)),
            pltpu.SemaphoreType.DMA((2, 3)),
            pltpu.SemaphoreType.DMA((2, 3)),
        ],
        compiler_params=pltpu.CompilerParams(
            collective_id=0, has_side_effects=True, vmem_limit_bytes=48 * 2**20
        ),
    )(x_start.reshape(NRHS * CELLS, 128), labels, conduct, electrodes)
    return out.reshape(x_start.shape)


def solution(mesh):
    return jax.shard_map(
        per_device,
        mesh=mesh,
        in_specs=(P(None, "gx", "gy", "gz"), P("gx", "gy", "gz"), P(), P()),
        out_specs=P(None, "gx", "gy", "gz"),
        check_vma=False,
    )
```

time: 610 us -> 81 us (0.13); the launches traced: 601 us -> 80.8 us
  blocking collectives: 383 us -> 0 us
  starting transfers between devices: 81.7 us -> 0 us
  Pallas kernels: 0 us -> 76.9 us
  other arithmetic: 56.3 us -> 0 us
  local copies, waits for them, and re-layouts: 36.3 us -> 3.89 us
  waiting for transfers between devices: 25.5 us -> 0 us
  matrix products: 16.6 us -> 0 us
    psum x5 -> x0, blocking collectives: 383 us -> none  [the longest x2 153 us: per_device(): curvature = lax.psum(local_gram(direction, image), ('gx', 'gy', 'gz'))]
    ppermute x30 -> x0, starting transfers between devices: 81.7 us -> none  [the longest x15 54 us: with_halo(): before = lax.ppermute(last, axis, up)]
    pallas_call x0 -> x1, Pallas kernels: none -> 76.9 us  [per_device(): pl.pallas_call(kernel, out_shape=jax.ShapeDtypeStruct((NRHS * CELLS, 128)...]
    another operation x25 -> x0, other arithmetic: 34.4 us -> none  [the longest x15 18.2 us: spd_solve(): lower = lax.linalg.cholesky(matrix)]
    ppermute x30 -> x0, waiting for transfers between devices: 25.5 us -> none  [the longest x15 20.5 us: with_halo(): after = lax.ppermute(leading, axis, down)]
    slice x22 -> x0, local copies, waits for them, and re-layouts: 14.9 us -> none  [the longest x13 10.2 us: with_halo(): last = lax.slice_in_dim(value, length - width, length, axis=dim)]
    dot_general x14 -> x0, matrix products: 14.4 us -> none  [the longest x7 7.09 us: combine(): jnp.dot(coeff.T, field.reshape(count, -1), precision=HIGH)]
    concatenate x16 -> x0, other arithmetic: 13.6 us -> none  [with_halo(): value = jnp.concatenate([before, value, after], axis=dim)]
  transfers between devices with their start and end apart: 30 -> 0, of which waited for: 13 -> 0; matrix products, arithmetic and copies ran while one was open for 5% -> 0% of each run, Pallas kernels for 0% -> 0%
where the time goes in v1:
time: 81 us; the launch traced here: 80.8 us
  Pallas kernels  76.9 us (95%)
  local copies, waits for them, and re-layouts  3.89 us (5%)
    pallas_call x1, Pallas kernels, per_device(): pl.pallas_call(kernel, out_shape=jax.ShapeDtypeStruct((NRHS * CELLS, 128)...  76.9 us
    unnamed x9, local copies, waits for them, and re-layouts  3.89 us

profile of v1, /device:TPU:1, one launch (start us, length us, event | category | flops | bytes accessed | tf_op | source)
XLA Modules:
  0.0 80.8 jit_solution(17654460534105317923)
XLA Ops:
  0.0 0.0 copy-start.3
  0.0 0.7 copy-done.3
  0.7 0.0 copy-start
  0.7 1.0 %copy-done = f32[32,2,16,128]{3,2,1,0:T(8,128)S(1)} copy-done((f32[32,2,16,128]{3,2,1,0:T(8,128)S(1)}, f32[32,2,16,128]{3,2,1,0:T(8,128)}, u32[]{:S(2)}) %copy-start) | copy-done | bytes 524312
  1.7 0.0 copy-start.1
  1.7 0.7 copy-done.1
  2.4 0.0 copy-start.2
  2.4 0.7 copy-done.2
  3.1 76.9 %shard_map.46 = f32[1024,128]{1,0:T(8,128)S(1)} custom-call(f32[1024,128]{1,0:T(8,128)S(1)} %bitcast.3, s32[2,16,128]{2,1,0:T(8,128)S(1)} %copy-done.1, f32[8,9]{1,0:T(8,128)S(1)} %copy-done.2, s32[33]{0:T(128)S(1)} %copy-done.3), custom_call_target="tpu_custom_call" | custom-call | tf_op jit(solution)/shard_map/pallas_call | solution.py:463
  80.0 0.8 copy.6
Async XLA Ops:
  0.0 0.7 copy-start.3
  0.7 1.0 %copy-start = (f32[32,2,16,128]{3,2,1,0:T(8,128)S(1)}, f32[32,2,16,128]{3,2,1,0:T(8,128)}, u32[]{:S(2)}) copy-start(f32[32,2,16,128]{3,2,1,0:T(8,128)} %param.4) | copy-start | bytes 1572868
  1.7 0.7 copy-start.1
  2.4 0.7 copy-start.2

commit v2 on v1

--- a/solution.py
+++ b/solution.py
@@ -25,6 +25,10 @@
 SIDE = tuple(o for o in NEAR if o[2] != 0)
 PLANE = tuple((0, b, c) for b in range(GY) for c in range(GZ) if b or c)
 LINE = tuple((2 * a, 0, 0) for a in range(1, GX // 2))
+UNROLL = 8
+GRAM = 8
+SECOND = 8
+FINISH = 8
 HALO_TILES = 90
 LABEL_TILES = 36
 
@@ -37,12 +41,6 @@
     return lax.axis_index("gx"), lax.axis_index("gy"), lax.axis_index("gz")
 
 
-def device(offset):
-    x, y, z = coordinates()
-    dx, dy, dz = wrapped(offset)
-    return (lax.rem(x + dx, GX), lax.rem(y + dy, GY), lax.rem(z + dz, GZ))
-
-
 def from_slot(offset, order):
     return order.index(tuple(-o for o in offset))
 
@@ -67,27 +65,29 @@
     return lax.broadcasted_iota(jnp.int32, shape, 0)
 
 
-def eliminate(matrix):
-    tiles = [matrix[8 * g : 8 * g + 8] for g in range(4)]
+def eliminate(matrices):
+    sets = [[m[8 * g : 8 * g + 8] for g in range(4)] for m in matrices]
     row = sublanes((8, 128))
     width = 8
     for start in range(0, NRHS, width):
-        columns = [
-            [jnp.broadcast_to(t[:, start + j : start + j + 1], (8, 128)) for t in tiles] for j in range(width)
+        panels = [
+            [[jnp.broadcast_to(t[:, start + j : start + j + 1], (8, 128)) for t in tiles] for j in range(width)]
+            for tiles in sets
         ]
         for j in range(width):
             own, inner = divmod(start + j, 8)
-            scale = 1.0 / columns[j][own][inner : inner + 1]
-            for which in [None] + list(range(j + 1, width)):
-                target = tiles if which is None else columns[which]
-                pivot = jnp.broadcast_to(target[own][inner : inner + 1] * scale, (8, 128))
-                new = [t - c * pivot for t, c in zip(target, columns[j])]
-                new[own] = jnp.where(row == inner, pivot, new[own])
-                if which is None:
-                    tiles = new
-                else:
-                    columns[which] = new
-    return jnp.concatenate(tiles, axis=0)
+            for index, columns in enumerate(panels):
+                scale = 1.0 / columns[j][own][inner : inner + 1]
+                for which in [None] + list(range(j + 1, width)):
+                    target = sets[index] if which is None else columns[which]
+                    pivot = jnp.broadcast_to(target[own][inner : inner + 1] * scale, (8, 128))
+                    new = [t - c * pivot for t, c in zip(target, columns[j])]
+                    new[own] = jnp.where(row == inner, pivot, new[own])
+                    if which is None:
+                        sets[index] = new
+                    else:
+                        columns[which] = new
+    return [jnp.concatenate(tiles, axis=0) for tiles in sets]
 
 
 def part(matrix, index):
@@ -104,10 +104,11 @@
 
 
 def kernel(
-    x_ref, label_ref, conduct, electrodes, out_ref,
-    f0, f1, f2, f3, f4, dirs, image, second,
+    x_in, label_in, conduct_in, electrodes_in, out_ref,
+    x_ref, label_ref, conduct, electrodes, in_sem,
+    f0, f1, f2, f3, f4, dirs, image,
     label_got, padded, rows, weights, side_weights,
-    pack0, pack1, pack2, pack3, got0, got1, got2, got3, ends,
+    pack0, pack1, pack2, pack3, got0, got1, got2, got3,
     give, plane_a, line_a, pair_a, mid_a, sum_a, plane_b, line_b, pair_b, mid_b, sum_b,
     dummy, halo_send, halo_recv, label_sem, red_send, red_recv,
 ):
@@ -117,10 +118,46 @@
     gx, gy, gz = coordinates()
     lane8 = lanes((8, 128))
 
+    copies = [
+        pltpu.make_async_copy(src, dst, in_sem.at[i])
+        for i, (src, dst) in enumerate(
+            ((x_in, x_ref), (label_in, label_ref), (conduct_in, conduct), (electrodes_in, electrodes))
+        )
+    ]
+    for copy in copies:
+        copy.start()
+
     partners = list(dict.fromkeys([wrapped(o) for o in NEAR] + list(PLANE) + list(LINE)))
+    along = [
+        {d: (c + d) & (n - 1) if d else c for d in sorted({p[a] for p in partners} | {0})}
+        for a, (c, n) in enumerate(((gx, GX), (gy, GY), (gz, GZ)))
+    ]
+
+    def device(offset):
+        return tuple(table[d] for table, d in zip(along, wrapped(offset)))
+
     barrier = pltpu.get_barrier_semaphore()
     for offset in partners:
         pl.semaphore_signal(barrier, inc=1, device_id=device(offset), device_id_type=MESH)
+
+    copies[0].wait()
+    for chunk in range(2):
+
+        def load(i, acc, chunk=chunk):
+            for inner in range(4):
+                y = 4 * i + inner
+                for x in range(CX):
+                    tile = x_ref[pl.ds(512 * chunk + CY * x + y, 16, stride=CELLS), :]
+                    f0[x + 1, y + 1, 16 * chunk : 16 * chunk + 16, :] = tile
+                    for half in range(2):
+                        spot = 32 * half + CY * x + y
+                        moved = pltpu.roll(tile[8 * half : 8 * half + 8], 2 * spot + 1, 1)
+                        acc = jnp.where(lane8 // 2 == spot, moved, acc)
+            return acc
+
+        pack0[chunk] = lax.fori_loop(0, CY // 4, load, jnp.zeros((8, 128), F32))
+    for copy in copies[1:]:
+        copy.wait()
     pl.semaphore_wait(barrier, len(partners))
 
     def put(src, dst, send, recv, offset):
@@ -138,17 +175,19 @@
         ys = {0: pl.ds(0, CY), 1: pl.ds(CY - 8, 8), -1: pl.ds(0, 8)}[dy]
         return ref.at[xs, ys]
 
-    for slot, offset in enumerate(NEAR):
-        put(label_part(label_ref, offset), label_part(label_got.at[slot], offset), label_sem.at[0], label_sem.at[1], offset)
-
-    def send(level, chunk):
+    x_from, x_to = {1: CX, -1: 1}, {1: 0, -1: CX + 1}
+    y_from, y_to = {1: CY, -1: 1}, {1: 0, -1: CY + 1}
+
+    def send_far(level, chunk):
+        field, r = fields[level], pl.ds(16 * chunk, 16)
+        ss, rs = halo_send.at[level, chunk], halo_recv.at[level, chunk]
+        for dx in (1, -1):
+            put(field.at[x_from[dx], 1 : CY + 1, r], field.at[x_to[dx], 1 : CY + 1, r], ss, rs, (dx, 0, 0))
+
+    def send_near(level, chunk):
         field, pack, got = fields[level], packs[level], gots[level]
         r = pl.ds(16 * chunk, 16)
         ss, rs = halo_send.at[level, chunk], halo_recv.at[level, chunk]
-        x_from, x_to = {1: CX, -1: 1}, {1: 0, -1: CX + 1}
-        y_from, y_to = {1: CY, -1: 1}, {1: 0, -1: CY + 1}
-        for dx in (1, -1):
-            put(field.at[x_from[dx], 1 : CY + 1, r], field.at[x_to[dx], 1 : CY + 1, r], ss, rs, (dx, 0, 0))
         for slot, offset in enumerate(SIDE):
             put(pack.at[chunk], got.at[slot, chunk], ss, rs, offset)
         for dy in (1, -1):
@@ -157,19 +196,15 @@
             for dy in (1, -1):
                 put(field.at[x_from[dx], y_from[dy], r], field.at[x_to[dx], y_to[dy], r], ss, rs, (dx, dy, 0))
 
-    for chunk in range(2):
-
-        def load(y, acc, chunk=chunk):
-            for x in range(CX):
-                tile = x_ref[pl.ds(512 * chunk + CY * x + y, 16, stride=CELLS), :]
-                f0[x + 1, y + 1, 16 * chunk : 16 * chunk + 16, :] = tile
-                for half in range(2):
-                    spot = 32 * half + CY * x + y
-                    acc = jnp.where(lane8 // 2 == spot, pltpu.roll(tile[8 * half : 8 * half + 8], 2 * spot + 1, 1), acc)
-            return acc
-
-        pack0[chunk] = lax.fori_loop(0, CY, load, jnp.zeros((8, 128), F32))
-        send(0, chunk)
+    def send(level, chunk):
+        send_far(level, chunk)
+        send_near(level, chunk)
+
+    send_far(0, 0)
+    for slot, offset in enumerate(NEAR):
+        put(label_part(label_ref, offset), label_part(label_got.at[slot], offset), label_sem.at[0], label_sem.at[1], offset)
+    send_near(0, 0)
+    send(0, 1)
 
     take(dummy.at[pl.ds(0, LABEL_TILES)], label_sem.at[1])
     lane16 = lanes((CY, 128))
@@ -272,45 +307,57 @@
         end = jnp.zeros((8, 128), F32)
         for f, cross in enumerate(CROSS):
             end = end + side_weights[f] * parts[cross]
-        ends[...] = end
-
-        def body(y, acc):
-            results = []
-            for x in range(CX):
-                c = CY * x + y
-                for half in range(2):
-                    r = pl.ds(base + 8 * half, 8)
-                    u = {
-                        (dx, dy): src[x + 1 + dx, y + 1 + dy, r, :] for dx in (-1, 0, 1) for dy in (-1, 0, 1)
-                    }
-                    value = weights[0, c] * u[0, 0]
-                    for i, offset in enumerate(FLAT):
-                        value = value - weights[1 + i, c] * u[offset[0], offset[1]]
-                    up = weights[9, c] * u[0, 0]
-                    down = weights[14, c] * u[0, 0]
-                    for f in range(1, 5):
-                        up = up + weights[9 + f, c] * u[CROSS[f]]
-                        down = down + weights[14 + f, c] * u[CROSS[f]]
-                    spot = 32 * half + c
-                    side = pltpu.roll(ends[...], 127 - 2 * spot, 1)
-                    up = jnp.where(lane8 == 0, side, up)
-                    down = jnp.where(lane8 == 127, side, down)
-                    value = value - pltpu.roll(up, 127, 1) - pltpu.roll(down, 1, 1)
-                    if level == 0:
-                        flat = flat_base + x * (GY * CY * GZ * CZ) + y * (GZ * CZ) + lane8
-                        hit = jnp.where(flat == wanted[2 * chunk + half], 40.0, 0.0)
-                        value = (hit - jnp.where(flat == common, 40.0, 0.0)) - value
-                    if level < 3:
-                        acc = jnp.where(lane8 // 2 == spot, pltpu.roll(value, 2 * spot + 1, 1), acc)
-                    results.append((x, r, value))
-            for x, r, value in results:
+
+        def body(i, acc):
+            held, loaded, results = {}, {}, []
+
+            def weight(index, c, key):
+                if (index, key) not in held:
+                    held[index, key] = weights[index, c]
+                return held[index, key]
+
+            def field(xx, inner, half):
+                if (xx, inner, half) not in loaded:
+                    loaded[xx, inner, half] = src[xx, UNROLL * i + inner, pl.ds(base + 8 * half, 8), :]
+                return loaded[xx, inner, half]
+
+            for inner in range(UNROLL):
+                y = UNROLL * i + inner
+                for x in range(CX):
+                    c = CY * x + y
+                    for half in range(2):
+                        key = (x, inner)
+                        u = {
+                            (dx, dy): field(x + 1 + dx, inner + 1 + dy, half) for dx in (-1, 0, 1) for dy in (-1, 0, 1)
+                        }
+                        value = weight(0, c, key) * u[0, 0]
+                        for k, offset in enumerate(FLAT):
+                            value = value - weight(1 + k, c, key) * u[offset[0], offset[1]]
+                        up = weight(9, c, key) * u[0, 0]
+                        down = weight(14, c, key) * u[0, 0]
+                        for f in range(1, 5):
+                            up = up + weight(9 + f, c, key) * u[CROSS[f]]
+                            down = down + weight(14 + f, c, key) * u[CROSS[f]]
+                        spot = 32 * half + c
+                        side = pltpu.roll(end, 127 - 2 * spot, 1)
+                        up = jnp.where(lane8 == 0, side, up)
+                        down = jnp.where(lane8 == 127, side, down)
+                        value = value - pltpu.roll(up, 127, 1) - pltpu.roll(down, 1, 1)
+                        if level == 0:
+                            flat = flat_base + x * (GY * CY * GZ * CZ) + y * (GZ * CZ) + lane8
+                            hit = jnp.where(flat == wanted[2 * chunk + half], 40.0, 0.0)
+                            value = (hit - jnp.where(flat == common, 40.0, 0.0)) - value
+                        if level < 3:
+                            acc = jnp.where(lane8 // 2 == spot, pltpu.roll(value, 2 * spot + 1, 1), acc)
+                        results.append((x, y, half, value))
+            for x, y, half, value in results:
                 if level == 3:
-                    dst[x, y, r, :] = value
+                    dst[x, y, pl.ds(base + 8 * half, 8), :] = value
                 else:
-                    dst[x + 1, y + 1, r, :] = value
+                    dst[x + 1, y + 1, pl.ds(base + 8 * half, 8), :] = value
             return acc
 
-        acc = lax.fori_loop(0, CY, body, jnp.zeros((8, 128), F32))
+        acc = lax.fori_loop(0, CY // UNROLL, body, jnp.zeros((8, 128), F32))
         if level < 3:
             packs[level + 1][chunk] = acc
 
@@ -321,8 +368,11 @@
     chip = gx // 2
 
     def plane_send(value, got, index):
-        give[index] = value.reshape(4, 8, 128)
-        got[mine] = value.reshape(4, 8, 128)
+        spare = value[24:32]
+        for g in range(3):
+            tile = jnp.where(lane8 < 96, value[8 * g : 8 * g + 8], pltpu.roll(spare, 96 - 32 * g, 1))
+            give[index, g] = tile
+            got[mine, g] = tile
         for offset in PLANE:
             put(give.at[index], got.at[mine], red_send.at[index, 0], red_recv.at[index, 0], offset)
 
@@ -349,27 +399,39 @@
 
     def pair_take(got, mid, index):
         take(got, red_recv.at[index, 2])
-        return (mid[1] + got[...]).reshape(NRHS, 128)
-
-    def field_rows(ref, y, inner):
+        tiles = [mid[1, g] + got[g] for g in range(3)]
+        spare = jnp.zeros((8, 128), F32)
+        for g in range(3):
+            spare = jnp.where(lane8 // 32 == g, pltpu.roll(tiles[g], (32 + 32 * g) % 128, 1), spare)
+        tiles = [jnp.where(lane8 < 96, tile, 0.0) for tile in tiles]
+        return jnp.concatenate(tiles + [spare], axis=0)
+
+    def field_rows(ref, i, count, inner):
         o = 1 if inner else 0
-        return jnp.concatenate([ref[x + o, 2 * y + j + o] for j in range(2) for x in range(CX)], axis=1)
-
-    for level in range(2):
-        for chunk in range(2):
-            arrived(level, chunk)
-            operate(level, chunk)
-            send(level + 1, chunk)
-
-    def gram_first(y, acc):
-        both = jnp.concatenate([field_rows(f1, y, True), field_rows(f2, y, True)], axis=0)
-        return acc + mm_nt(both, both)
-
-    both = lax.fori_loop(0, CY // 2, gram_first, jnp.zeros((64, 64), F32))
-    wide = jnp.concatenate([both, jnp.zeros((64, 64), F32)], axis=1)
+        return jnp.concatenate([ref[x + o, count * i + j + o] for j in range(count) for x in range(CX)], axis=1)
+
+    for chunk in range(2):
+        arrived(0, chunk)
+        operate(0, chunk)
+        send(1, chunk)
+
+    def gram_zero(i, acc):
+        v0 = field_rows(f1, i, GRAM, True)
+        return acc + mm_nt(v0, v0)
+
+    m0 = lax.fori_loop(0, CY // GRAM, gram_zero, jnp.zeros((NRHS, NRHS), F32))
+    for chunk in range(2):
+        arrived(1, chunk)
+        operate(1, chunk)
+        send(2, chunk)
+
+    def gram_first(i, acc):
+        v0, u1 = field_rows(f1, i, GRAM, True), field_rows(f2, i, GRAM, True)
+        return acc + mm_nt(u1, jnp.concatenate([v0, u1], axis=0))
+
+    first = lax.fori_loop(0, CY // GRAM, gram_first, jnp.zeros((NRHS, 64), F32))
+    first = jnp.concatenate([m0, first, jnp.zeros((NRHS, 32), F32)], axis=1)
     lane32 = lanes((NRHS, 128))
-    first = jnp.where(lane32 < 64, wide[:NRHS], pltpu.roll(wide[NRHS:], 32, 1))
-    first = jnp.where(lane32 < 96, first, 0.0)
     plane_send(first, plane_a, 0)
 
     arrived(2, 0)
@@ -384,57 +446,63 @@
     operate(3, 0)
     sums = pair_take(pair_a, mid_a, 0)
 
-    solved = eliminate(pltpu.roll(sums, 96, 1))
+    solved, inverse = eliminate([pltpu.roll(sums, 96, 1), sums])
     alpha0 = part(solved, 3)
     turn0 = mm(part(solved, 1), alpha0)
     eye = jnp.where(sublanes((NRHS, NRHS)) == lanes((NRHS, NRHS)), 1.0, 0.0)
     beta0 = turn0 - eye
     rho1 = mm(part(sums, 0), beta0)
-    mix = jnp.concatenate([turn0, -alpha0], axis=0)
+    back0 = mm(part(inverse, 1), beta0)
+    mix = jnp.concatenate([turn0, -alpha0], axis=0).T
 
     arrived(3, 1)
     operate(3, 1)
 
-    def second_block(y, acc):
-        v0, u1 = field_rows(f1, y, True), field_rows(f2, y, True)
-        u2, u3 = field_rows(f3, y, True), field_rows(f4, y, False)
+    def second_block(i, acc):
+        v0, u1 = field_rows(f1, i, SECOND, True), field_rows(f2, i, SECOND, True)
+        u2, u3 = field_rows(f3, i, SECOND, True), field_rows(f4, i, SECOND, False)
         top = jnp.concatenate([v0, u1, u2], axis=1)
         low = jnp.concatenate([u1, u2, u3], axis=1)
-        new = mm_t(mix, jnp.concatenate([top, low], axis=0))
-        p1, q1, aq1 = new[:, :512], new[:, 512:1024], new[:, 1024:]
-        dirs[y] = p1
-        image[y] = q1
-        return acc + mm_nt(q1, jnp.concatenate([p1, q1, aq1, u1], axis=0))
-
-    grams = lax.fori_loop(0, CY // 2, second_block, jnp.zeros((NRHS, 128), F32))
+        new = mm(mix, jnp.concatenate([top, low], axis=0))
+        n = 256 * SECOND
+        p1, q1, aq1 = new[:, :n], new[:, n : 2 * n], new[:, 2 * n :]
+        for j in range(SECOND):
+            dirs[SECOND * i + j] = p1[:, 256 * j : 256 * j + 256]
+            image[SECOND * i + j] = q1[:, 256 * j : 256 * j + 256]
+        return acc + mm_nt(q1, jnp.concatenate([p1, q1, aq1], axis=0))
+
+    grams = lax.fori_loop(0, CY // SECOND, second_block, jnp.zeros((NRHS, 96), F32))
+    grams = jnp.concatenate([grams, jnp.zeros((NRHS, 32), F32)], axis=1)
     plane_send(grams, plane_b, 1)
     line_send(plane_b, line_b, mid_b, 1)
     pair_send(line_b, pair_b, mid_b, 1)
     sums = pair_take(pair_b, mid_b, 1)
 
     wide_rho = jnp.concatenate([rho1, jnp.zeros((NRHS, 96), F32)], axis=1)
-    solved = eliminate(jnp.where(lane32 < 64, sums, pltpu.roll(wide_rho, 64, 1)))
+    solved = eliminate([jnp.where(lane32 < 64, sums, pltpu.roll(wide_rho, 64, 1))])[0]
     alpha1 = part(solved, 2)
     turn1 = mm(part(solved, 1), alpha1)
-    qq, qaq, qu = part(sums, 1), part(sums, 2), part(sums, 3)
-    gram2 = mm_t(alpha1, mm(qaq, alpha1) + mm(qu, beta0) - mm(qq, turn1))
+    gram1, qq, qaq = part(sums, 0), part(sums, 1), part(sums, 2)
+    gram2 = mm_t(alpha1, mm(qaq, alpha1) - mm(gram1, back0) - mm(qq, turn1))
     rho2 = mm(rho1, turn1 - eye)
-    solved = eliminate(jnp.concatenate([gram2, rho2, jnp.zeros((NRHS, 64), F32)], axis=1))
+    solved = eliminate([jnp.concatenate([gram2, rho2, jnp.zeros((NRHS, 64), F32)], axis=1)])[0]
     alpha2 = part(solved, 1)
     last = jnp.concatenate(
         [alpha0 - mm(beta0, alpha2), alpha1 + mm(turn1, alpha2), -mm(alpha1, alpha2)], axis=0
-    )
-
-    def finish(y, carry):
-        update = mm_t(last, jnp.concatenate([field_rows(f1, y, True), dirs[y], image[y]], axis=0))
-        for j in range(2):
+    ).T
+
+    def finish(i, carry):
+        old = [field_rows(f1, i, FINISH, True)]
+        old += [jnp.concatenate([ref[FINISH * i + j] for j in range(FINISH)], axis=1) for ref in (dirs, image)]
+        update = mm(last, jnp.concatenate(old, axis=0))
+        for j in range(FINISH):
             for x in range(CX):
                 piece = update[:, 128 * (2 * j + x) : 128 * (2 * j + x) + 128]
-                value = f0[x + 1, 2 * y + j + 1] + piece
-                out_ref[pl.ds(CY * x + 2 * y + j, NRHS, stride=CELLS), :] = value
+                value = f0[x + 1, FINISH * i + j + 1] + piece
+                out_ref[pl.ds(CY * x + FINISH * i + j, NRHS, stride=CELLS), :] = value
         return carry
 
-    lax.fori_loop(0, CY // 2, finish, 0)
+    lax.fori_loop(0, CY // FINISH, finish, 0)
 
     take(dummy.at[pl.ds(0, LABEL_TILES)], label_sem.at[0])
     for level in range(4):
@@ -448,25 +516,31 @@
 
 def per_device(x_start, labels, conduct, electrodes):
     vmem = pl.BlockSpec(memory_space=pltpu.VMEM)
-    smem = pl.BlockSpec(memory_space=pltpu.SMEM)
     field = pltpu.VMEM((CX + 2, CY + 2, NRHS, 128), F32)
-    half = pltpu.VMEM((CY // 2, NRHS, 512), F32)
+    half = pltpu.VMEM((CY, NRHS, 256), F32)
     pack = pltpu.VMEM((2, 8, 128), F32)
     got = pltpu.VMEM((10, 2, 8, 128), F32)
     reduce = [
-        pltpu.VMEM((16, 4, 8, 128), F32),
-        pltpu.VMEM((8, 4, 8, 128), F32),
-        pltpu.VMEM((4, 8, 128), F32),
-        pltpu.VMEM((2, 4, 8, 128), F32),
-        pltpu.VMEM((4, 8, 128), F32),
+        pltpu.VMEM((16, 3, 8, 128), F32),
+        pltpu.VMEM((8, 3, 8, 128), F32),
+        pltpu.VMEM((3, 8, 128), F32),
+        pltpu.VMEM((2, 3, 8, 128), F32),
+        pltpu.VMEM((3, 8, 128), F32),
     ]
     out = pl.pallas_call(
         kernel,
         out_shape=jax.ShapeDtypeStruct((NRHS * CELLS, 128), F32),
-        in_specs=[vmem, vmem, smem, smem],
+        in_specs=[pl.BlockSpec(memory_space=pltpu.HBM)] * 4,
         out_specs=vmem,
-        scratch_shapes=[field] * 4
-        + [pltpu.VMEM((CX, CY, NRHS, 128), F32), half, half, half]
+        scratch_shapes=[
+            pltpu.VMEM((NRHS * CELLS, 128), F32),
+            pltpu.VMEM((CX, CY, 128), jnp.int32),
+            pltpu.SMEM((LABELS, 9), F32),
+            pltpu.SMEM((NRHS + 1,), jnp.int32),
+            pltpu.SemaphoreType.DMA((4,)),
+        ]
+        + [field] * 4
+        + [pltpu.VMEM((CX, CY, NRHS, 128), F32), half, half]
         + [
             pltpu.VMEM((18, CX, CY, 128), jnp.int32),
             pltpu.VMEM((3, CX + 2, 32, 128), jnp.int32),
@@ -476,7 +550,7 @@
         ]
         + [pack] * 4
         + [got] * 4
-        + [pltpu.VMEM((8, 128), F32), pltpu.VMEM((2, 4, 8, 128), F32)]
+        + [pltpu.VMEM((2, 3, 8, 128), F32)]
         + reduce * 2
         + [
             pltpu.VMEM((HALO_TILES, 8, 128), F32),

time: 81 us -> 64.8 us (0.80)
  Pallas kernels: 76.9 us -> 60.7 us
    pallas_call x1, Pallas kernels: 76.9 us -> 60.7 us  [per_device(): pl.pallas_call(kernel, out_shape=jax.ShapeDtypeStruct((NRHS * CELLS, 128)...]
where the time goes in v2:
time: 64.8 us; the launch traced here: 64.6 us
  Pallas kernels  60.7 us (94%)
  local copies, waits for them, and re-layouts  3.89 us (6%)
    pallas_call x1, Pallas kernels, per_device(): pl.pallas_call(kernel, out_shape=jax.ShapeDtypeStruct((NRHS * CELLS, 128)...  60.7 us
    unnamed x9, local copies, waits for them, and re-layouts  3.89 us

profile of v2, /device:TPU:1, one launch (start us, length us, event | category | flops | bytes accessed | tf_op | source)
XLA Modules:
  0.0 64.6 jit_solution(10558765113430063341)
XLA Ops:
  0.0 0.0 copy-start.3
  0.0 0.7 %copy-done.3 = s32[33]{0:T(128)S(1)} copy-done((s32[33]{0:T(128)S(1)}, s32[33]{0:T(128)}, u32[]{:S(2)}) %copy-start.3) | copy-done | bytes 156
  0.7 0.0 copy-start
  0.7 1.0 %copy-done = f32[32,2,16,128]{3,2,1,0:T(8,128)S(1)} copy-done((f32[32,2,16,128]{3,2,1,0:T(8,128)S(1)}, f32[32,2,16,128]{3,2,1,0:T(8,128)}, u32[]{:S(2)}) %copy-start) | copy-done | bytes 524312
  1.7 0.0 copy-start.1
  1.7 0.7 %copy-done.1 = s32[2,16,128]{2,1,0:T(8,128)S(1)} copy-done((s32[2,16,128]{2,1,0:T(8,128)S(1)}, s32[2,16,128]{2,1,0:T(8,128)}, u32[]{:S(2)}) %copy-start.1) | copy-done | bytes 16408
  2.4 0.0 copy-start.2
  2.4 0.7 %copy-done.2 = f32[8,9]{1,0:T(8,128)S(1)} copy-done((f32[8,9]{1,0:T(8,128)S(1)}, f32[8,9]{1,0:T(8,128)}, u32[]{:S(2)}) %copy-start.2) | copy-done | bytes 312
  3.1 60.7 %shard_map.46 = f32[1024,128]{1,0:T(8,128)S(1)} custom-call(f32[1024,128]{1,0:T(8,128)S(1)} %bitcast.3, s32[2,16,128]{2,1,0:T(8,128)S(1)} %copy-done.1, f32[8,9]{1,0:T(8,128)S(1)} %copy-done.2, s32[33]{0:T(128)S(1)} %copy-done.3), custom_call_target="tpu_custom_call" | custom-call | tf_op jit(solution)/shard_map/pallas_call | solution.py:530
  63.8 0.8 %copy.6 = f32[32,2,16,128]{3,2,1,0:T(8,128)} copy(f32[32,2,16,128]{3,2,1,0:T(8,128)S(1)} %bitcast.2) | data formatting | bytes 1048576
Async XLA Ops:
  0.0 0.7 %copy-start.3 = (s32[33]{0:T(128)S(1)}, s32[33]{0:T(128)}, u32[]{:S(2)}) copy-start(s32[33]{0:T(128)} %electrodes_in.1) | copy-start | bytes 400
  0.7 1.0 %copy-start = (f32[32,2,16,128]{3,2,1,0:T(8,128)S(1)}, f32[32,2,16,128]{3,2,1,0:T(8,128)}, u32[]{:S(2)}) copy-start(f32[32,2,16,128]{3,2,1,0:T(8,128)} %param.4) | copy-start | bytes 1572868
  1.7 0.7 %copy-start.1 = (s32[2,16,128]{2,1,0:T(8,128)S(1)}, s32[2,16,128]{2,1,0:T(8,128)}, u32[]{:S(2)}) copy-start(s32[2,16,128]{2,1,0:T(8,128)} %label_in.1) | copy-start | bytes 49156
  2.4 0.7 %copy-start.2 = (f32[8,9]{1,0:T(8,128)S(1)}, f32[8,9]{1,0:T(8,128)}, u32[]{:S(2)}) copy-start(f32[8,9]{1,0:T(8,128)} %conduct_in.1) | copy-start | bytes 868

commit v3 on v2

--- a/solution.py
+++ b/solution.py
@@ -51,6 +51,17 @@
 
 def mm_t(a, b):
     return lax.dot_general(a, b, (((0,), (0,)), ((), ())), precision=HIGH, preferred_element_type=F32)
+
+
+def split(a):
+    high = a.astype(jnp.bfloat16)
+    return high, (a - high.astype(F32)).astype(jnp.bfloat16)
+
+
+def mm_three(a, b):
+    (a_high, a_low), (b_high, b_low) = split(a), split(b)
+    total = jnp.dot(a_high, b_low, preferred_element_type=F32) + jnp.dot(a_low, b_high, preferred_element_type=F32)
+    return total + jnp.dot(a_high, b_high, preferred_element_type=F32)
 
 
 def mm_nt(a, b):
@@ -200,14 +211,14 @@
         send_far(level, chunk)
         send_near(level, chunk)
 
-    send_far(0, 0)
     for slot, offset in enumerate(NEAR):
         put(label_part(label_ref, offset), label_part(label_got.at[slot], offset), label_sem.at[0], label_sem.at[1], offset)
+    send_far(0, 0)
     send_near(0, 0)
     send(0, 1)
 
+    owns = [[lookup(label_ref[x], conduct, kind) for kind in range(9)] for x in range(CX)]
     take(dummy.at[pl.ds(0, LABEL_TILES)], label_sem.at[1])
-    lane16 = lanes((CY, 128))
     inside = {
         (0, 1): gx < GX - 1, (0, -1): gx > 0, (1, 1): gy < GY - 1, (1, -1): gy > 0, (2, 1): gz < GZ - 1, (2, -1): gz > 0,
     }
@@ -243,8 +254,7 @@
                 put_rows(shift, xx, dx, -1)
 
     for x in range(CX):
-        here = padded[1, x + 1, 8:24, :]
-        own = [lookup(here, conduct, kind) for kind in range(9)]
+        own = owns[x]
         total = jnp.zeros((CY, 128), F32)
         for offset in NEAR:
             dx, dy, dz = offset
@@ -434,16 +444,15 @@
     lane32 = lanes((NRHS, 128))
     plane_send(first, plane_a, 0)
 
-    arrived(2, 0)
-    operate(2, 0)
-    send(3, 0)
+    for chunk in range(2):
+        arrived(2, chunk)
+        operate(2, chunk)
+        send(3, chunk)
     line_send(plane_a, line_a, mid_a, 0)
-    arrived(2, 1)
-    operate(2, 1)
-    send(3, 1)
+    for chunk in range(2):
+        arrived(3, chunk)
+        operate(3, chunk)
     pair_send(line_a, pair_a, mid_a, 0)
-    arrived(3, 0)
-    operate(3, 0)
     sums = pair_take(pair_a, mid_a, 0)
 
     solved, inverse = eliminate([pltpu.roll(sums, 96, 1), sums])
@@ -454,9 +463,6 @@
     rho1 = mm(part(sums, 0), beta0)
     back0 = mm(part(inverse, 1), beta0)
     mix = jnp.concatenate([turn0, -alpha0], axis=0).T
-
-    arrived(3, 1)
-    operate(3, 1)
 
     def second_block(i, acc):
         v0, u1 = field_rows(f1, i, SECOND, True), field_rows(f2, i, SECOND, True)
@@ -494,7 +500,7 @@
     def finish(i, carry):
         old = [field_rows(f1, i, FINISH, True)]
         old += [jnp.concatenate([ref[FINISH * i + j] for j in range(FINISH)], axis=1) for ref in (dirs, image)]
-        update = mm(last, jnp.concatenate(old, axis=0))
+        update = mm_three(last, jnp.concatenate(old, axis=0))
         for j in range(FINISH):
             for x in range(CX):
                 piece = update[:, 128 * (2 * j + x) : 128 * (2 * j + x) + 128]

time: 64.8 us -> 63.5 us (0.980)
  Pallas kernels: 60.7 us -> 59.4 us
    pallas_call x1, Pallas kernels: 60.7 us -> 59.4 us  [per_device(): pl.pallas_call(kernel, out_shape=jax.ShapeDtypeStruct((NRHS * CELLS, 128)...]
where the time goes in v3:
time: 63.5 us; the launch traced here: 63.3 us
  Pallas kernels  59.4 us (94%)
  local copies, waits for them, and re-layouts  3.89 us (6%)
    pallas_call x1, Pallas kernels, per_device(): pl.pallas_call(kernel, out_shape=jax.ShapeDtypeStruct((NRHS * CELLS, 128)...  59.4 us
    unnamed x9, local copies, waits for them, and re-layouts  3.89 us

profile of v3, /device:TPU:1, one launch (start us, length us, event | category | flops | bytes accessed | tf_op | source)
XLA Modules:
  0.0 63.3 jit_solution(10647296551962014368)
XLA Ops:
  0.0 0.0 copy-start.3
  0.0 0.7 %copy-done.3 = s32[33]{0:T(128)S(1)} copy-done((s32[33]{0:T(128)S(1)}, s32[33]{0:T(128)}, u32[]{:S(2)}) %copy-start.3) | copy-done | bytes 156
  0.7 0.0 copy-start
  0.7 1.0 %copy-done = f32[32,2,16,128]{3,2,1,0:T(8,128)S(1)} copy-done((f32[32,2,16,128]{3,2,1,0:T(8,128)S(1)}, f32[32,2,16,128]{3,2,1,0:T(8,128)}, u32[]{:S(2)}) %copy-start) | copy-done | bytes 524312
  1.7 0.0 copy-start.1
  1.7 0.7 %copy-done.1 = s32[2,16,128]{2,1,0:T(8,128)S(1)} copy-done((s32[2,16,128]{2,1,0:T(8,128)S(1)}, s32[2,16,128]{2,1,0:T(8,128)}, u32[]{:S(2)}) %copy-start.1) | copy-done | bytes 16408
  2.4 0.0 copy-start.2
  2.4 0.7 %copy-done.2 = f32[8,9]{1,0:T(8,128)S(1)} copy-done((f32[8,9]{1,0:T(8,128)S(1)}, f32[8,9]{1,0:T(8,128)}, u32[]{:S(2)}) %copy-start.2) | copy-done | bytes 312
  3.1 59.4 %shard_map.46 = f32[1024,128]{1,0:T(8,128)S(1)} custom-call(f32[1024,128]{1,0:T(8,128)S(1)} %bitcast.3, s32[2,16,128]{2,1,0:T(8,128)S(1)} %copy-done.1, f32[8,9]{1,0:T(8,128)S(1)} %copy-done.2, s32[33]{0:T(128)S(1)} %copy-done.3), custom_call_target="tpu_custom_call" | custom-call | tf_op jit(solution)/shard_map/pallas_call | solution.py:536
  62.5 0.8 %copy.6 = f32[32,2,16,128]{3,2,1,0:T(8,128)} copy(f32[32,2,16,128]{3,2,1,0:T(8,128)S(1)} %bitcast.2) | data formatting | bytes 1048576
Async XLA Ops:
  0.0 0.7 %copy-start.3 = (s32[33]{0:T(128)S(1)}, s32[33]{0:T(128)}, u32[]{:S(2)}) copy-start(s32[33]{0:T(128)} %electrodes_in.1) | copy-start | bytes 400
  0.7 1.0 %copy-start = (f32[32,2,16,128]{3,2,1,0:T(8,128)S(1)}, f32[32,2,16,128]{3,2,1,0:T(8,128)}, u32[]{:S(2)}) copy-start(f32[32,2,16,128]{3,2,1,0:T(8,128)} %param.4) | copy-start | bytes 1572868
  1.7 0.7 %copy-start.1 = (s32[2,16,128]{2,1,0:T(8,128)S(1)}, s32[2,16,128]{2,1,0:T(8,128)}, u32[]{:S(2)}) copy-start(s32[2,16,128]{2,1,0:T(8,128)} %label_in.1) | copy-start | bytes 49156
  2.4 0.7 %copy-start.2 = (f32[8,9]{1,0:T(8,128)S(1)}, f32[8,9]{1,0:T(8,128)}, u32[]{:S(2)}) copy-start(f32[8,9]{1,0:T(8,128)} %conduct_in.1) | copy-start | bytes 868

commit v4 on v3

--- a/solution.py
+++ b/solution.py
@@ -79,7 +79,7 @@
 def eliminate(matrices):
     sets = [[m[8 * g : 8 * g + 8] for g in range(4)] for m in matrices]
     row = sublanes((8, 128))
-    width = 8
+    width = 16
     for start in range(0, NRHS, width):
         panels = [
             [[jnp.broadcast_to(t[:, start + j : start + j + 1], (8, 128)) for t in tiles] for j in range(width)]
@@ -189,11 +189,11 @@
     x_from, x_to = {1: CX, -1: 1}, {1: 0, -1: CX + 1}
     y_from, y_to = {1: CY, -1: 1}, {1: 0, -1: CY + 1}
 
-    def send_far(level, chunk):
+    def send_far(level, chunk, ys=slice(1, CY + 1)):
         field, r = fields[level], pl.ds(16 * chunk, 16)
         ss, rs = halo_send.at[level, chunk], halo_recv.at[level, chunk]
         for dx in (1, -1):
-            put(field.at[x_from[dx], 1 : CY + 1, r], field.at[x_to[dx], 1 : CY + 1, r], ss, rs, (dx, 0, 0))
+            put(field.at[x_from[dx], ys, r], field.at[x_to[dx], ys, r], ss, rs, (dx, 0, 0))
 
     def send_near(level, chunk):
         field, pack, got = fields[level], packs[level], gots[level]
@@ -367,7 +367,11 @@
                     dst[x + 1, y + 1, pl.ds(base + 8 * half, 8), :] = value
             return acc
 
-        acc = lax.fori_loop(0, CY // UNROLL, body, jnp.zeros((8, 128), F32))
+        acc = jnp.zeros((8, 128), F32)
+        for i in range(CY // UNROLL):
+            acc = body(i, acc)
+            if level < 3:
+                send_far(level + 1, chunk, slice(UNROLL * i + 1, UNROLL * (i + 1) + 1))
         if level < 3:
             packs[level + 1][chunk] = acc
 
@@ -423,7 +427,7 @@
     for chunk in range(2):
         arrived(0, chunk)
         operate(0, chunk)
-        send(1, chunk)
+        send_near(1, chunk)
 
     def gram_zero(i, acc):
         v0 = field_rows(f1, i, GRAM, True)
@@ -433,7 +437,7 @@
     for chunk in range(2):
         arrived(1, chunk)
         operate(1, chunk)
-        send(2, chunk)
+        send_near(2, chunk)
 
     def gram_first(i, acc):
         v0, u1 = field_rows(f1, i, GRAM, True), field_rows(f2, i, GRAM, True)
@@ -447,7 +451,7 @@
     for chunk in range(2):
         arrived(2, chunk)
         operate(2, chunk)
-        send(3, chunk)
+        send_near(3, chunk)
     line_send(plane_a, line_a, mid_a, 0)
     for chunk in range(2):
         arrived(3, chunk)

time: 63.5 us -> 62.2 us (0.980)
  Pallas kernels: 59.4 us -> 58.1 us
    pallas_call x1, Pallas kernels: 59.4 us -> 58.1 us  [per_device(): pl.pallas_call(kernel, out_shape=jax.ShapeDtypeStruct((NRHS * CELLS, 128)...]
where the time goes in v4:
time: 62.2 us; the launch traced here: 62 us
  Pallas kernels  58.1 us (93%)
  local copies, waits for them, and re-layouts  3.89 us (6%)
    pallas_call x1, Pallas kernels, per_device(): pl.pallas_call(kernel, out_shape=jax.ShapeDtypeStruct((NRHS * CELLS, 128)...  58.1 us
    unnamed x9, local copies, waits for them, and re-layouts  3.89 us

profile of v4, /device:TPU:1, one launch (start us, length us, event | category | flops | bytes accessed | tf_op | source)
XLA Modules:
  0.0 62.0 jit_solution(4783089589548395825)
XLA Ops:
  0.0 0.0 copy-start.3
  0.0 0.7 %copy-done.3 = s32[33]{0:T(128)S(1)} copy-done((s32[33]{0:T(128)S(1)}, s32[33]{0:T(128)}, u32[]{:S(2)}) %copy-start.3) | copy-done | bytes 156
  0.7 0.0 copy-start
  0.7 1.0 %copy-done = f32[32,2,16,128]{3,2,1,0:T(8,128)S(1)} copy-done((f32[32,2,16,128]{3,2,1,0:T(8,128)S(1)}, f32[32,2,16,128]{3,2,1,0:T(8,128)}, u32[]{:S(2)}) %copy-start) | copy-done | bytes 524312
  1.7 0.0 copy-start.1
  1.7 0.7 %copy-done.1 = s32[2,16,128]{2,1,0:T(8,128)S(1)} copy-done((s32[2,16,128]{2,1,0:T(8,128)S(1)}, s32[2,16,128]{2,1,0:T(8,128)}, u32[]{:S(2)}) %copy-start.1) | copy-done | bytes 16408
  2.4 0.0 copy-start.2
  2.4 0.7 %copy-done.2 = f32[8,9]{1,0:T(8,128)S(1)} copy-done((f32[8,9]{1,0:T(8,128)S(1)}, f32[8,9]{1,0:T(8,128)}, u32[]{:S(2)}) %copy-start.2) | copy-done | bytes 312
  3.1 58.1 %shard_map.46 = f32[1024,128]{1,0:T(8,128)S(1)} custom-call(f32[1024,128]{1,0:T(8,128)S(1)} %bitcast.3, s32[2,16,128]{2,1,0:T(8,128)S(1)} %copy-done.1, f32[8,9]{1,0:T(8,128)S(1)} %copy-done.2, s32[33]{0:T(128)S(1)} %copy-done.3), custom_call_target="tpu_custom_call" | custom-call | tf_op jit(solution)/shard_map/pallas_call | solution.py:540
  61.2 0.8 %copy.6 = f32[32,2,16,128]{3,2,1,0:T(8,128)} copy(f32[32,2,16,128]{3,2,1,0:T(8,128)S(1)} %bitcast.2) | data formatting | bytes 1048576
Async XLA Ops:
  0.0 0.7 %copy-start.3 = (s32[33]{0:T(128)S(1)}, s32[33]{0:T(128)}, u32[]{:S(2)}) copy-start(s32[33]{0:T(128)} %electrodes_in.1) | copy-start | bytes 400
  0.7 1.0 %copy-start = (f32[32,2,16,128]{3,2,1,0:T(8,128)S(1)}, f32[32,2,16,128]{3,2,1,0:T(8,128)}, u32[]{:S(2)}) copy-start(f32[32,2,16,128]{3,2,1,0:T(8,128)} %param.4) | copy-start | bytes 1572868
  1.7 0.7 %copy-start.1 = (s32[2,16,128]{2,1,0:T(8,128)S(1)}, s32[2,16,128]{2,1,0:T(8,128)}, u32[]{:S(2)}) copy-start(s32[2,16,128]{2,1,0:T(8,128)} %label_in.1) | copy-start | bytes 49156
  2.4 0.7 %copy-start.2 = (f32[8,9]{1,0:T(8,128)S(1)}, f32[8,9]{1,0:T(8,128)}, u32[]{:S(2)}) copy-start(f32[8,9]{1,0:T(8,128)} %conduct_in.1) | copy-start | bytes 868
